TPU v7x, 32 devices: a whole 2x2x4 slice. The times are simulated.
32 devices in a mesh: tok: 16 (over z, x, core), mlp: 2 (over y).
Axes of the slice: x: 2, y: 2, z: 4, core: 2. Of those that a mesh axis runs over, the one named last changes fastest.
Arguments:
- queries: bfloat16 [1024, 7168], P('tok', 'mlp')
- fresh_token_keys: bfloat16 [1024, 1024], P('tok', 'mlp'), may hold values from -6 to 6
- fresh_token_values: bfloat16 [1024, 1024], P('tok', 'mlp'), may hold values from -6 to 6
- leaf_key_block: bfloat16 [5120, 1024], P('tok', 'mlp'), may hold values from -6 to 6
- leaf_value_block: bfloat16 [5120, 1024], P('tok', 'mlp'), may hold values from -6 to 6
- shared_key_block: bfloat16 [4096, 1024], P('tok', 'mlp'), may hold values from -6 to 6
- shared_value_block: bfloat16 [4096, 1024], P('tok', 'mlp'), may hold values from -6 to 6
- out_weight: bfloat16 [7168, 7168], P('mlp', 'tok'), may hold values from -0.0625 to 0.0625
- residual: bfloat16 [1024, 7168], P('mlp', 'tok'), may hold values from -2.5 to 2.5
- token_request: int32 [1024], replicated, may hold values from 0 to 15, as said below
- positions: int32 [1024], P('tok'), may hold values from 129 to 831, as said below
- parents: int32 [26], replicated, may hold values from -1 to 9, as said below
- node_lengths: int32 [26], replicated, may hold values from 1 to 256, as said below
- node_owner: int32 [26], replicated, may hold values from 0 to 15, as said below
Outputs:
- hidden: bfloat16 [1024, 7168], P('mlp', 'tok')
- leaf_key_output: bfloat16 [5120, 1024], P('tok', 'mlp')
- leaf_value_output: bfloat16 [5120, 1024], P('tok', 'mlp')
Inputs may be any that keep to these rules, and one draw needn't show every extreme that they name: `token_request`: index d of tok holds the 64 new tokens of the request whose leaf it owns (node_owner of that leaf is d), in some order. positions = node_lengths of the token's root, middle and leaf plus the token's rank among its request's new tokens; the ranks of one request are 0 to 63, each once. `parents`: nodes 0 to 1 are roots (parent -1), the next 8 are middle nodes with a root as parent, the last 16 are the leaves of requests 0, 1, ... with a middle node as parent; every root and middle node has a child; the leaf of request 0 lies below root 0. `node_lengths`: roots and middle nodes hold 64 to 256 tokens, root 0 and the middle node above leaf 0 exactly 256; leaves hold 1 to 256, leaf 0 exactly 256. `node_owner`: the 10 roots and middle nodes have different owners; the leaves' owners are a permutation of the indices of tok; a node's cache starts at row 0 of its owner's block.
All inputs are finite; a program needn't handle non-finite values.
Results may differ from a plain program's by a relative error of at most 0.012.
Values may be sent and summed in bfloat16 or wider, within the bound.
A program may use at most 64 MiB of HBM per device.

v0:
```python
import math

import jax
import jax.numpy as jnp
from jax import lax
from jax.sharding import PartitionSpec as P

HEAD_SIZE = 128
ROOTS = 2
MIDS = 8


THETA = 5000000.0
NEG = -1e30


def apply_rotary(values, position, heads):
    width = values.shape[1] // heads
    half = width // 2
    table = values.astype(jnp.float32).reshape(values.shape[0], heads, width)
    freq = THETA ** (-(jnp.arange(half, dtype=jnp.float32) * 2.0) / width)
    angle = position.astype(jnp.float32)[:, None] * freq[None, :]
    cosine = jnp.cos(angle)[:, None, :]
    sine = jnp.sin(angle)[:, None, :]
    first = table[:, :, :half]
    second = table[:, :, half:]
    turned = jnp.concatenate(
        [first * cosine - second * sine, second * cosine + first * sine], axis=2
    )
    return turned.reshape(values.shape).astype(jnp.bfloat16)


def attend_key_block(queries4, keys, values, valid):
    scale = 1.0 / math.sqrt(queries4.shape[-1])
    scores = (
        jnp.einsum("sgqd,rgd->sgqr", queries4, keys, preferred_element_type=jnp.float32) * scale
    )
    allowed = valid[:, None, None, :]
    highest = jnp.max(jnp.where(allowed, scores, NEG), axis=3)
    weights = jnp.where(allowed, jnp.exp(scores - highest[..., None]), 0.0).astype(jnp.bfloat16)
    total = jnp.sum(weights.astype(jnp.float32), axis=3)
    output = jnp.einsum("sgqr,rgd->sgqd", weights, values, preferred_element_type=jnp.float32)
    return (highest, total, output)


def merge_state(state, block):
    high_a, total_a, out_a = state
    running_peak_b, running_sum_b, partial_output_b = block
    highest = jnp.maximum(high_a, running_peak_b)
    scale_a = jnp.exp(high_a - highest)
    scale_b = jnp.exp(running_peak_b - highest)
    return (
        highest,
        scale_a * total_a + scale_b * running_sum_b,
        scale_a[..., None] * out_a + scale_b[..., None] * partial_output_b,
    )


def lookup(table, index):
    return jnp.sum(jnp.where(jnp.arange(table.shape[0]) == index, table, 0))


def body(
    queries,
    fresh_token_keys,
    fresh_token_values,
    leaf_key_block,
    leaf_value_block,
    shared_key_block,
    shared_value_block,
    out_weight,
    residual,
    token_request,
    positions,
    parents,
    node_lengths,
    node_owner,
):
    my_index = lax.axis_index("tok")
    tok_rows = queries.shape[0]
    width = HEAD_SIZE
    q_heads = queries.shape[1] // width
    kv_heads = fresh_token_keys.shape[1] // width
    group = q_heads // kv_heads
    kv_width = kv_heads * width
    shared_count = ROOTS + MIDS
    query_turned = apply_rotary(queries, positions, q_heads)
    key_turned = apply_rotary(fresh_token_keys, positions, kv_heads)
    my_request = lax.dynamic_slice_in_dim(token_request, my_index * tok_rows, 1)[0]
    leaf_node = shared_count + my_request
    middle = lookup(parents, leaf_node)
    root = lookup(parents, middle)
    leaf_length = lookup(node_lengths, leaf_node)
    root_length = lookup(node_lengths, root)
    middle_length = lookup(node_lengths, middle)
    new_index = positions - root_length - middle_length - leaf_length
    leaf_rows = leaf_key_block.shape[0]
    row_ids = jnp.arange(leaf_rows)
    place = (row_ids[:, None] == (leaf_length + new_index)[None, :]).astype(jnp.bfloat16)
    pairs = jnp.concatenate([key_turned, fresh_token_values], axis=1)
    placed = jnp.dot(place, pairs, preferred_element_type=jnp.float32).astype(jnp.bfloat16)
    keep = row_ids[:, None] < leaf_length
    leaf_key_output = jnp.where(keep, leaf_key_block, placed[:, :kv_width])
    leaf_value_output = jnp.where(keep, leaf_value_block, placed[:, kv_width:])
    token_queries = query_turned.reshape(tok_rows, kv_heads, group, width)
    leaf_row_mask = row_ids[None, :] < (leaf_length + new_index + 1)[:, None]
    leaf_state = attend_key_block(
        token_queries,
        leaf_key_output.reshape(leaf_rows, kv_heads, width),
        leaf_value_output.reshape(leaf_rows, kv_heads, width),
        leaf_row_mask,
    )
    node_rows = shared_key_block.shape[0]
    root_owner = lookup(node_owner, root)
    middle_owner = lookup(node_owner, middle)
    gathered = (
        lax.all_gather(shared_key_block, "tok", axis=0, tiled=True),
        lax.all_gather(shared_value_block, "tok", axis=0, tiled=True),
    )
    root_keys = lax.dynamic_slice_in_dim(gathered[0], root_owner * node_rows, node_rows, 0)
    root_values = lax.dynamic_slice_in_dim(gathered[1], root_owner * node_rows, node_rows, 0)
    middle_keys = lax.dynamic_slice_in_dim(gathered[0], middle_owner * node_rows, node_rows, 0)
    middle_values = lax.dynamic_slice_in_dim(gathered[1], middle_owner * node_rows, node_rows, 0)
    node_ids = jnp.arange(node_rows)
    both_keys = jnp.concatenate([root_keys, middle_keys], axis=0).reshape(
        2 * node_rows, kv_heads, width
    )
    both_values = jnp.concatenate([root_values, middle_values], axis=0).reshape(
        2 * node_rows, kv_heads, width
    )
    both_valid = jnp.concatenate([node_ids < root_length, node_ids < middle_length], axis=0)
    shared_state = attend_key_block(token_queries, both_keys, both_values, both_valid[None, :])
    final = merge_state(shared_state, leaf_state)
    attended_local = (
        (final[2] / final[1][..., None]).reshape(tok_rows, q_heads * width).astype(jnp.bfloat16)
    )
    projected = jnp.dot(
        lax.all_gather(attended_local, "tok", axis=0, tiled=True),
        out_weight,
        preferred_element_type=jnp.float32,
    )
    summed = lax.psum_scatter(projected, "mlp", scatter_dimension=0, tiled=True)
    hidden = (residual.astype(jnp.float32) + summed).astype(jnp.bfloat16)
    return (hidden, leaf_key_output, leaf_value_output)


def solution(mesh):
    placed = (
        P("tok", "mlp"),
        P("tok", "mlp"),
        P("tok", "mlp"),
        P("tok", "mlp"),
        P("tok", "mlp"),
        P("tok", "mlp"),
        P("tok", "mlp"),
        P("mlp", "tok"),
        P("mlp", "tok"),
        P(),
        P("tok"),
        P(),
        P(),
        P(),
    )
    return jax.shard_map(
        body,
        mesh=mesh,
        in_specs=placed,
        out_specs=(P("mlp", "tok"), P("tok", "mlp"), P("tok", "mlp")),
        check_vma=False,
    )
```

profile of v0, /device:TPU:0, one launch (start us, length us, event | category | flops | bytes accessed | tf_op | source)
XLA Modules:
  0.0 239.5 jit_solution(10957576545156087570)
XLA Ops:
  7.2 1.9 copy.21
  9.2 1.8 copy.25
  11.1 1.3 dynamic_slice.15
  13.0 1.3 fusion.24
  14.3 1.9 select_reduce_fusion.2
  16.3 2.7 %fusion.25 = (s32[]{:T(128)}, s32[]{:T(128)}, s32[]{:T(128)}, s32[]{:T(128)}, s32[]{:T(128)}) fusion(s32[26]{0:T(128)} %param.26, s32[]{:T(128)} %bitcast, s32[]{:T(128)} %select_reduce_fusion.2, s32[]{:T(128)} %fusion.24, s32[26]{0:T(128)} %param.27), kind=kLoop, calls=%fused_computation.63 | loop fusion | flops 333 | bytes 240 | tf_op jit(solution)/shard_map/reduce_sum | solution.py:60
  20.2 0.9 reshape.153
  21.1 2.0 broadcast_add_fusion
  24.3 1.2 convolution_convert_fusion
  25.4 1.9 slice_select_fusion
  27.4 0.8 reshape.149
  28.2 1.1 reshape.147
  29.3 2.3 reshape.151
  31.6 2.2 subtract_convert_fusion
  34.1 0.9 copy.22
  37.1 1.7 fusion.4
  38.8 1.6 copy-done.1
  40.4 1.0 convert_reduce_fusion.1
  41.4 24.7 %all-gather.4.cloned.1.call-done = bf16[4096,512]{0,1:T(8,128)(2,1)} async-done(((bf16[256,512]{0,1:T(8,128)(2,1)}), bf16[4096,512]{0,1:T(8,128)(2,1)}) %all-gather.4.cloned.1.call-update) | async-done | bytes 4194320 | tf_op jit(solution)/shard_map/all_gather | solution.py:117
  66.1 1.1 constant_dynamic-slice_fusion.3
  68.0 51.7 %all-gather.6.cloned.1.call-done = bf16[4096,512]{0,1:T(8,128)(2,1)} async-done(((bf16[256,512]{0,1:T(8,128)(2,1)}), bf16[4096,512]{0,1:T(8,128)(2,1)}) %all-gather.6.cloned.1.call-update) | async-done | bytes 4194320 | tf_op jit(solution)/shard_map/all_gather | solution.py:118
  119.7 1.1 constant_dynamic-slice_fusion.1
  120.8 2.0 fusion
  122.9 1.0 convert_reduce_fusion
  123.9 0.9 fusion.11
  124.9 1.2 fusion.12
  126.0 1.1 copy.28
  127.1 2.3 convert_element_type.53
  129.5 66.6 %all-gather.8.cloned.1.call-done = bf16[1024,3584]{1,0:T(8,128)(2,1)} async-done(((bf16[64,3584]{1,0:T(8,128)(2,1)}), bf16[1024,3584]{1,0:T(8,128)(2,1)}) %all-gather.8.cloned.1.call-update) | async-done | bytes 7340048 | tf_op jit(solution)/shard_map/all_gather | solution.py:138
  196.1 7.1 %fusion.35 = f32[1024,448]{0,1:T(8,128)} fusion(bf16[1024,3584]{1,0:T(8,128)(2,1)} %all-gather.8.cloned.1.call-done, bf16[3584,448]{0,1:T(8,128)(2,1)S(1)} %copy-done), kind=kOutput, calls=%fused_computation.78 | convolution fusion | flops 3288334336 | bytes 12386304 | tf_op jit(solution)/shard_map/dot_general | solution.py:137
  203.2 27.5 %reduce-scatter.2.cloned.1.call-done = f32[512,448]{0,1:T(8,128)} async-done(((f32[1024,448]{0,1:T(8,128)}), f32[512,448]{0,1:T(8,128)}) %reduce-scatter.2.cloned.1.call-update) | async-done | bytes 917520 | tf_op jit(solution)/shard_map/reduce_scatter | solution.py:142
  230.7 2.2 add_convert_fusion.1
  (41 shorter events, 4.6 us)
Async XLA Ops:
  7.2 188.9 %copy-start = (bf16[3584,448]{0,1:T(8,128)(2,1)S(1)}, bf16[3584,448]{0,1:T(8,128)(2,1)}, u32[]{:S(2)}) copy-start(bf16[3584,448]{0,1:T(8,128)(2,1)} %param.21) | copy-start | bytes 9633796
  7.2 58.9 %all-gather.4.cloned.1.call-start = ((), (), s32[]{:S(2)}) async-start(), calls=%async_computation.1 | async-start | bytes 4456448 | tf_op jit(solution)/shard_map/all_gather | solution.py:117
  9.2 110.5 %all-gather.6.cloned.1.call-start = ((), (), s32[]{:S(2)}) async-start(), calls=%async_computation.2 | async-start | bytes 4456448 | tf_op jit(solution)/shard_map/all_gather | solution.py:118
  11.0 185.0 %all-gather.8.cloned.1.call-start = ((), (), s32[]{:S(2)}) async-start(), calls=%async_computation.3 | async-start | bytes 7798784 | tf_op jit(solution)/shard_map/all_gather | solution.py:138
  23.3 0.9 copy-start.5
  23.3 0.9 copy-start.6
  27.4 0.9 copy-start.3
  37.1 1.7 copy-start.7
  38.8 1.6 copy-start.1
  40.4 80.4 %copy-start.9 = (pred[512]{0:T(512)(128)(4,1)S(1)}, pred[512]{0:T(512)(128)(4,1)}, u32[]{:S(2)}) copy-start(pred[512]{0:T(512)(128)(4,1)} %pad_add_fusion) | copy-start | bytes 1540
  120.8 3.1 %copy-start.2 = (f32[4,320,64,7]{1,2,3,0:T(8,128)S(1)}, f32[4,320,64,7]{1,2,3,0:T(8,128)}, u32[]{:S(2)}) copy-start(f32[4,320,64,7]{1,2,3,0:T(8,128)} %copy-done.1) | copy-start | bytes 6881284
  120.8 3.1 %copy-start.4 = (bf16[320,4,128]{2,1,0:T(4,128)(2,1)S(1)}, bf16[320,4,128]{2,1,0:T(4,128)(2,1)}, u32[]{:S(2)}) copy-start(bf16[320,4,128]{2,1,0:T(4,128)(2,1)} %reshape.149) | copy-start | bytes 983044
  120.8 3.1 %copy-start.8 = (pred[64,320]{1,0:T(8,128)(4,1)S(1)}, pred[64,320]{1,0:T(8,128)(4,1)}, u32[]{:S(2)}) copy-start(pred[64,320]{1,0:T(8,128)(4,1)} %copy-done.7) | copy-start | bytes 61444
  129.5 101.3 %reduce-scatter.2.cloned.1.call-start = ((), (), s32[]{:S(2)}) async-start(), calls=%async_computation.4 | async-start | bytes 2752512 | tf_op jit(solution)/shard_map/reduce_scatter | solution.py:142
Sparse Core Ops, SparseCore 0:
  10.2 55.9 all-gather.3
  68.3 51.3 all-gather.5
  129.6 66.4 all-gather.7
  203.3 27.3 reduce-scatter.1
where the time goes:
time: 240 us; the launch traced here: 239 us
  waiting for transfers between devices  171 us (71%)
  other arithmetic  20.6 us (9%)
  local copies, waits for them, and re-layouts  18.3 us (8%)
  between operations  15.9 us (7%)
  matrix products  14 us (6%)
    all_gather x1, waiting for transfers between devices, body(): lax.all_gather(attended_local, 'tok', axis=0, tiled=True)  66.6 us
    all_gather x1, waiting for transfers between devices, body(): lax.all_gather(shared_value_block, 'tok', axis=0, tiled=True)  51.7 us
    reduce_scatter x1, waiting for transfers between devices, body(): summed = lax.psum_scatter(projected, 'mlp', scatter_dimension=0, tiled=True)  27.5 us
    all_gather x1, waiting for transfers between devices, body(): lax.all_gather(shared_key_block, 'tok', axis=0, tiled=True)  24.7 us
    dot_general x1, matrix products, body(): jnp.dot(lax.all_gather(attended_local, 'tok', axis=0, tiled=True), out_we...  7.09 us
    reduce_sum x3, other arithmetic, lookup(): return jnp.sum(jnp.where(jnp.arange(table.shape[0]) == index, table, 0))  5.94 us
    unnamed x23, local copies, waits for them, and re-layouts  5.39 us
  transfers between devices with their start and end apart: 4, of which 4 were waited for; matrix products, arithmetic and copies ran while one was open for 13% of the time, Pallas kernels for 0%

commit v1 on v0

v1 whole, which is shorter than its diff:
```python
import functools
import math

import jax
import jax.numpy as jnp
import numpy as np
from jax import lax
from jax.experimental import pallas as pl
from jax.experimental.pallas import tpu as pltpu
from jax.sharding import PartitionSpec as P

HEAD_SIZE = 128
ROOTS = 2
MIDS = 8
THETA = 5000000.0
NEG = -1e30
LEVELS = 4
ORDER = ((0, 1, 2, 3), (1, 0, 2, 3), (2, 3, 1, 0), (3, 2, 1, 0))
MESH = pl.DeviceIdType.MESH


def kernel(
    N, M,
    queries, fresh_k, fresh_v, leaf_k, leaf_v, shared_k, shared_v, weight, residual,
    freq, request, pos, parents, lengths, owners,
    hidden, leaf_k_out, leaf_v_out,
    kv, att, w, qrot, own_acc, sums, out_sums, in_sums,
    kv_recv, kv_up, kv_down, kv_side, kv_core,
    at_recv, at_up, at_down, at_side, at_core,
    sum_send, sum_recv, local,
):
    t = lax.axis_index("tok")
    y = lax.axis_index("mlp")
    B = N // (2 * LEVELS)
    a, b, c = t // (2 * B), (t // 2) % B, t % 2
    rows = queries.shape[0]
    heads = kv.shape[3] // HEAD_SIZE
    group = queries.shape[1] // HEAD_SIZE // heads
    gw = group * HEAD_SIZE

    def tid(a_, b_, c_):
        return (a_ * B + b_) * 2 + c_

    def level(k):
        code = sum(ORDER[i][k] * 4**i for i in range(LEVELS))
        return (code // jnp.where(a == 0, 1, jnp.where(a == 1, 4, jnp.where(a == 2, 16, 64)))) % 4

    barrier = pltpu.get_barrier_semaphore()

    def greet(dev):
        pl.semaphore_signal(barrier, inc=1, device_id=dev, device_id_type=MESH)

    @pl.when(a > 0)
    def _():
        greet((tid(a - 1, b, c), y))

    @pl.when(a < LEVELS - 1)
    def _():
        greet((tid(a + 1, b, c), y))

    for j in range(1, B):
        greet((tid(a, (b + j) % B, c), y))
    greet((tid(a, b, 1 - c), y))
    for j in range(1, M):
        greet((t, (y + j) % M))

    loads = [
        pltpu.make_async_copy(shared_k, kv.at[0, t], local.at[0]),
        pltpu.make_async_copy(shared_v, kv.at[1, t], local.at[1]),
        pltpu.make_async_copy(weight, w, local.at[2]),
    ]
    for load in loads:
        load.start()
    pl.semaphore_wait(
        barrier, B + M - 1 + jnp.minimum(a, 1) + jnp.minimum(LEVELS - 1 - a, 1)
    )

    def copy(src, dst, ss, rs, dev):
        return pltpu.make_async_remote_copy(
            src_ref=src, dst_ref=dst, send_sem=ss, recv_sem=rs,
            device_id=(dev, y), device_id_type=MESH,
        )

    def stage1(buf, recv, up, down, side, core, k, it, src=None, go=True):
        L = level(k)
        slot = tid(L, b, c)
        dst = buf.at[it, slot]
        rs = recv.at[it, slot]
        if go and k > 0:
            copy(dst, dst, core.at[k, it, 0], rs, tid(a, b, 1 - c)).wait_recv()
        src = dst if src is None else src
        act = (lambda d: d.start()) if go else (lambda d: d.wait_send())

        @pl.when(jnp.logical_and(L <= a, a < LEVELS - 1))
        def _():
            act(copy(src, dst, up.at[k, it], rs, tid(a + 1, b, c)))

        @pl.when(jnp.logical_and(L >= a, a > 0))
        def _():
            act(copy(src, dst, down.at[k, it], rs, tid(a - 1, b, c)))

        for j in range(1, B):
            act(copy(src, dst, side.at[k, it, j - 1], rs, tid(a, (b + j) % B, c)))
        act(copy(src, dst, core.at[k, it, 0], rs, tid(a, b, 1 - c)))

    def stage2(buf, recv, up, down, side, core, k, it, go=True):
        L = level(k)
        for j in range(1, B):
            slot = tid(L, (b + j) % B, c)
            d = copy(
                buf.at[it, slot], buf.at[it, slot], core.at[k, it, j],
                recv.at[it, slot], tid(a, b, 1 - c),
            )
            if go:
                d.wait_recv()
                d.start()
            else:
                d.wait_send()

    def stage3(buf, recv, up, down, side, core, k, it):
        L = level(k)
        for j in range(B):
            slot = tid(L, (b + j) % B, 1 - c)
            copy(
                buf.at[it, slot], buf.at[it, slot], core.at[k, it, j],
                recv.at[it, slot], tid(a, b, 1 - c),
            ).wait_recv()

    kvs = (kv, kv_recv, kv_up, kv_down, kv_side, kv_core)
    ats = (att, at_recv, at_up, at_down, at_side, at_core)
    own = (shared_k, shared_v)

    stage1(*kvs, 0, 0, shared_k)
    stage1(*kvs, 0, 1, shared_v)

    leaf = ROOTS + MIDS + request[t * rows]
    middle = parents[leaf]
    root = parents[middle]
    leaf_length = lengths[leaf]
    root_length = lengths[root]
    middle_length = lengths[middle]
    prefix = root_length + middle_length
    eye = lax.broadcasted_iota(jnp.int32, (rows, rows), 0) == lax.broadcasted_iota(
        jnp.int32, (rows, rows), 1
    )
    pos_row = pos[...]
    pos_column = jnp.sum(
        jnp.where(eye, pos_row.astype(jnp.float32), 0.0), axis=1, keepdims=True
    )
    angle = pos_column * freq[...]
    cosine = jnp.cos(angle)
    lane = lax.broadcasted_iota(jnp.int32, (rows, HEAD_SIZE), 1)
    sine = jnp.where(lane < HEAD_SIZE // 2, -1.0, 1.0) * jnp.sin(angle)

    def turn(block):
        block = block.astype(jnp.float32)
        return (block * cosine + pltpu.roll(block, HEAD_SIZE // 2, 1) * sine).astype(jnp.bfloat16)

    for g in range(heads):
        for h in range(group):
            at = (g * group + h) * HEAD_SIZE
            qrot[g, h * rows : (h + 1) * rows, :] = turn(queries[:, at : at + HEAD_SIZE])

    leaf_rows = leaf_k.shape[0]
    row_ids = lax.broadcasted_iota(jnp.int32, (leaf_rows, rows), 0)
    place = jnp.where(row_ids == pos_row - prefix, 1.0, 0.0).astype(jnp.bfloat16)
    keep = lax.broadcasted_iota(jnp.int32, (leaf_rows, HEAD_SIZE), 0) < leaf_length
    for g in range(heads):
        s = slice(g * HEAD_SIZE, (g + 1) * HEAD_SIZE)
        pair = jnp.concatenate([turn(fresh_k[:, s]), fresh_v[:, s]], axis=1)
        put = jnp.dot(place, pair, preferred_element_type=jnp.float32)
        leaf_k_out[:, s] = jnp.where(
            keep, leaf_k[:, s].astype(jnp.float32), put[:, :HEAD_SIZE]
        ).astype(jnp.bfloat16)
        leaf_v_out[:, s] = jnp.where(
            keep, leaf_v[:, s].astype(jnp.float32), put[:, HEAD_SIZE:]
        ).astype(jnp.bfloat16)

    items = [(k, it) for k in range(LEVELS) for it in range(2)]
    for i in range(2, len(items) + 1):
        if i < len(items):
            stage1(*kvs, *items[i])
        if i == 2:
            stage2(*kvs, *items[0])
        stage2(*kvs, *items[i - 1])
    for item in items:
        stage3(*kvs, *item)
    loads[0].wait()
    loads[1].wait()

    node_rows = shared_k.shape[0]
    root_owner = owners[root]
    middle_owner = owners[middle]
    node_ids = lax.broadcasted_iota(jnp.int32, (1, node_rows), 1)
    shared_bias = jnp.concatenate(
        [
            jnp.where(node_ids < root_length, 0.0, NEG),
            jnp.where(node_ids < middle_length, 0.0, NEG),
        ],
        axis=1,
    )
    limit = jnp.concatenate([pos_column - (prefix - 1).astype(jnp.float32)] * group, axis=0)
    leaf_ids = lax.broadcasted_iota(jnp.int32, (1, leaf_rows), 1).astype(jnp.float32)
    factor = math.log2(math.e) / math.sqrt(HEAD_SIZE)
    ones = jnp.ones((2 * node_rows + leaf_rows, HEAD_SIZE), jnp.bfloat16)
    contract = (((1,), (1,)), ((), ()))

    def attend(g):
        s = slice(g * HEAD_SIZE, (g + 1) * HEAD_SIZE)
        q = qrot[g]
        shared_keys = jnp.concatenate([kv[0, root_owner, :, s], kv[0, middle_owner, :, s]], axis=0)
        values = jnp.concatenate(
            [kv[1, root_owner, :, s], kv[1, middle_owner, :, s], leaf_v_out[:, s]], axis=0
        )
        s1 = lax.dot_general(q, shared_keys, contract, preferred_element_type=jnp.float32)
        s2 = lax.dot_general(q, leaf_k_out[:, s], contract, preferred_element_type=jnp.float32)
        s1 = s1 + shared_bias
        s2 = jnp.where(leaf_ids < limit, s2, NEG)
        highest = jnp.maximum(
            jnp.max(s1, axis=1, keepdims=True), jnp.max(s2, axis=1, keepdims=True)
        )
        p = jnp.concatenate(
            [
                jnp.exp2((s1 - highest) * factor).astype(jnp.bfloat16),
                jnp.exp2((s2 - highest) * factor).astype(jnp.bfloat16),
            ],
            axis=1,
        )
        o = jnp.dot(
            p, jnp.concatenate([values, ones], axis=1), preferred_element_type=jnp.float32
        )
        o = (o[:, :HEAD_SIZE] / o[:, HEAD_SIZE:]).astype(jnp.bfloat16)
        for h in range(group):
            att[g, t, :, h * HEAD_SIZE : (h + 1) * HEAD_SIZE] = o[h * rows : (h + 1) * rows, :]

    for g in range(heads):
        attend(g)
        stage1(*ats, 0, g)

    loads[2].wait()
    pieces = N // 4
    per_level = pieces // LEVELS
    share = pieces // M

    def piece(k, i):
        return level(k) * per_level + i

    def sum_copy(k, i):
        p = piece(k, i)
        return pltpu.make_async_remote_copy(
            src_ref=out_sums.at[k * per_level + i], dst_ref=in_sums.at[y, p % share],
            send_sem=sum_send.at[k * per_level + i], recv_sem=sum_recv.at[y, p % share],
            device_id=(t, p // share), device_id_type=MESH,
        )

    def project(k, g):
        for i in range(per_level):
            p = piece(k, i)
            block = att[g, pl.ds(p * 4, 4)].reshape(4 * rows, gw)
            part = jnp.dot(
                block, w[g * gw : (g + 1) * gw, :], preferred_element_type=jnp.float32
            )
            if g > 0:
                part = sums[i] + part
            if g < heads - 1:
                sums[i] = part
                continue

            @pl.when(p // share == y)
            def _():
                own_acc[p % share] = part

            @pl.when(p // share != y)
            def _():
                out_sums[k * per_level + i] = part.astype(jnp.bfloat16)
                sum_copy(k, i).start()

    items = [(k, g) for k in range(LEVELS) for g in range(heads)]
    n = len(items)
    for i in range(n + 3):
        if heads <= i < n:
            stage1(*ats, *items[i])
        if 0 <= i - 1 < n:
            stage2(*ats, *items[i - 1])
        if 0 <= i - 3 < n:
            stage3(*ats, *items[i - 3])
            project(*items[i - 3])

    total = residual[...].astype(jnp.float32) + own_acc[...].reshape(residual.shape)
    for j in range(1, M):
        other = (y + j) % M
        for r in range(share):
            pltpu.make_async_remote_copy(
                src_ref=in_sums.at[other, r], dst_ref=in_sums.at[other, r],
                send_sem=sum_send.at[0], recv_sem=sum_recv.at[other, r],
                device_id=(t, other), device_id_type=MESH,
            ).wait_recv()
        total = total + in_sums[other].astype(jnp.float32).reshape(residual.shape)
    hidden[...] = total.astype(jnp.bfloat16)

    for k in range(LEVELS):
        for it in range(2):
            stage1(*kvs, k, it, own[it] if k == 0 else None, go=False)
            stage2(*kvs, k, it, go=False)
        for g in range(heads):
            stage1(*ats, k, g, go=False)
            stage2(*ats, k, g, go=False)
        for i in range(per_level):

            @pl.when(piece(k, i) // share != y)
            def _():
                sum_copy(k, i).wait_send()


def body(
    N, M,
    queries, fresh_k, fresh_v, leaf_k, leaf_v, shared_k, shared_v, weight, residual,
    request, positions, parents, lengths, owners,
):
    rows, q_width = queries.shape
    kv_width = fresh_k.shape[1]
    heads = kv_width // HEAD_SIZE
    group = q_width // kv_width
    half = HEAD_SIZE // 2
    B = N // (2 * LEVELS)
    columns = weight.shape[1]
    pieces = N // 4
    per_level = pieces // LEVELS
    share = pieces // M
    exponent = np.tile(np.arange(half, dtype=np.float64) * 2.0 / HEAD_SIZE, 2)
    freq = jnp.asarray((THETA**-exponent)[None, :].astype(np.float32))
    vmem = pl.BlockSpec(memory_space=pltpu.VMEM)
    anywhere = pl.BlockSpec(memory_space=pl.ANY)
    smem = pl.BlockSpec(memory_space=pltpu.SMEM)
    dma = pltpu.SemaphoreType.DMA
    bf16, f32 = jnp.bfloat16, jnp.float32

    def semaphores(items):
        return [
            dma((items, N)), dma((LEVELS, items)), dma((LEVELS, items)),
            dma((LEVELS, items, B - 1)), dma((LEVELS, items, B)),
        ]

    return pl.pallas_call(
        functools.partial(kernel, N, M),
        out_shape=(
            jax.ShapeDtypeStruct(residual.shape, bf16),
            jax.ShapeDtypeStruct(leaf_k.shape, bf16),
            jax.ShapeDtypeStruct(leaf_v.shape, bf16),
        ),
        in_specs=[vmem] * 5 + [anywhere] * 3 + [vmem] * 2 + [smem, vmem] + [smem] * 3,
        out_specs=(vmem, vmem, vmem),
        scratch_shapes=[
            pltpu.VMEM((2, N) + shared_k.shape, bf16),
            pltpu.VMEM((heads, N, rows, group * HEAD_SIZE), bf16),
            pltpu.VMEM(weight.shape, bf16),
            pltpu.VMEM((heads, group * rows, HEAD_SIZE), bf16),
            pltpu.VMEM((share, 4 * rows, columns), f32),
            pltpu.VMEM((per_level, 4 * rows, columns), f32),
            pltpu.VMEM((pieces, 4 * rows, columns), bf16),
            pltpu.VMEM((M, share, 4 * rows, columns), bf16),
        ]
        + semaphores(2)
        + semaphores(heads)
        + [dma((pieces,)), dma((M, share)), dma((3,))],
        compiler_params=pltpu.CompilerParams(
            collective_id=0, has_side_effects=True, vmem_limit_bytes=56 * 1024 * 1024
        ),
    )(
        queries, fresh_k, fresh_v, leaf_k, leaf_v, shared_k, shared_v, weight, residual,
        freq, request, positions.reshape(1, rows), parents, lengths, owners,
    )


def solution(mesh):
    both = P("tok", "mlp")
    return jax.shard_map(
        functools.partial(body, mesh.shape["tok"], mesh.shape["mlp"]),
        mesh=mesh,
        in_specs=(both,) * 7 + (P("mlp", "tok"),) * 2 + (P(), P("tok"), P(), P(), P()),
        out_specs=(P("mlp", "tok"), both, both),
        check_vma=False,
    )
```

time: 240 us -> 125 us (0.52)
  waiting for transfers between devices: 171 us -> 0 us
  Pallas kernels: 0 us -> 111 us
  other arithmetic: 20.6 us -> 0 us
  between operations: 15.9 us -> 0.64 us
  matrix products: 14 us -> 0 us
  local copies, waits for them, and re-layouts: 18.3 us -> 13.2 us
    all_gather x3 -> x0, waiting for transfers between devices: 143 us -> none  [the longest x1 66.6 us: body(): lax.all_gather(attended_local, 'tok', axis=0, tiled=True)]
    pallas_call x0 -> x1, Pallas kernels: none -> 111 us  [body(): pl.pallas_call(functools.partial(kernel, N, M), out_shape=(jax.ShapeDtype...]
    reduce_scatter x1 -> x0, waiting for transfers between devices: 27.5 us -> none  [body(): summed = lax.psum_scatter(projected, 'mlp', scatter_dimension=0, tiled=True)]
    dot_general x6 -> x0, matrix products: 14 us -> none  [the longest x1 7.09 us: body(): jnp.dot(lax.all_gather(attended_local, 'tok', axis=0, tiled=True), out_we...]
    reduce_sum x5 -> x0, other arithmetic: 7.91 us -> none  [the longest x3 5.94 us: lookup(): return jnp.sum(jnp.where(jnp.arange(table.shape[0]) == index, table, 0))]
    unnamed x23 -> x4, local copies, waits for them, and re-layouts: 5.39 us -> 11.2 us
    reshape x4 -> x0, local copies, waits for them, and re-layouts: 5.11 us -> none  [the longest x2 3.21 us: apply_rotary(): table = values.astype(jnp.float32).reshape(values.shape[0], heads, width)]
    dynamic_slice x3 -> x0, local copies, waits for them, and re-layouts: 3.41 us -> none  [the longest x1 1.27 us: body(): lax.dynamic_slice_in_dim(token_request, my_index * tok_rows, 1)[0]]
  transfers between devices with their start and end apart: 4 -> 0, of which waited for: 4 -> 0; matrix products, arithmetic and copies ran while one was open for 13% -> 0% of each run, Pallas kernels for 0% -> 0%
where the time goes in v1:
time: 125 us
  Pallas kernels  111 us (89%)
  local copies, waits for them, and re-layouts  13.2 us (11%)
    pallas_call x1, Pallas kernels, body(): pl.pallas_call(functools.partial(kernel, N, M), out_shape=(jax.ShapeDtype...  111 us
    unnamed x4, local copies, waits for them, and re-layouts  11.2 us

profile of v1, /device:TPU:0, one launch (start us, length us, event | category | flops | bytes accessed | tf_op | source)
XLA Modules:
  0.0 124.8 jit_solution(13473780017505056272)
XLA Ops:
  0.6 2.0 %copy.19.residual = bf16[512,448]{1,0:T(8,128)(2,1)} copy(bf16[512,448]{0,1:T(8,128)(2,1)} %param.23) | data formatting | bytes 917504 | tf_op args[8]
  2.7 5.7 %copy.18.weight = bf16[3584,448]{1,0:T(8,128)(2,1)} copy(bf16[3584,448]{0,1:T(8,128)(2,1)} %param.22) | data formatting | bytes 6422528 | tf_op args[7]
  8.4 110.9 %shard_map.166 = (bf16[512,448]{1,0:T(8,128)(2,1)}, bf16[320,512]{1,0:T(8,128)(2,1)}, bf16[320,512]{1,0:T(8,128)(2,1)}) custom-call(bf16[64,3584]{1,0:T(8,128)(2,1)} %queries.1, bf16[64,512]{1,0:T(8,128)(2,1)} %fresh_k.1, bf16[64,512]{1,0:T(8,128)(2,1)} %fresh_v.1, bf16[320,512]{1,0:T(8,128)(2,1)} %leaf_k.1, bf16[320,512]{1,0:T(8,128)(2,1)} %leaf_v.1, ...), custom_call_target="tpu_custom_call" | custom-call | tf_op jit(solution)/shard_map/pallas_call | solution.py:344
  119.4 2.0 %copy.20 = bf16[512,448]{0,1:T(8,128)(2,1)} copy(bf16[512,448]{1,0:T(8,128)(2,1)} %get-tuple-element.3) | data formatting | bytes 917504 | tf_op jit(solution)/shard_map/pallas_call | solution.py:344
  121.4 1.7 %copy.23 = bf16[320,512]{1,0:T(8,128)(2,1)} copy(bf16[320,512]{1,0:T(8,128)(2,1)} %get-tuple-element.10) | data formatting | bytes 655360
  123.1 1.7 %copy.24 = bf16[320,512]{1,0:T(8,128)(2,1)} copy(bf16[320,512]{1,0:T(8,128)(2,1)} %get-tuple-element.11) | data formatting | bytes 655360

commit v2 on v1

--- a/solution.py
+++ b/solution.py
@@ -25,8 +25,8 @@
     freq, request, pos, parents, lengths, owners,
     hidden, leaf_k_out, leaf_v_out,
     kv, att, w, qrot, own_acc, sums, out_sums, in_sums,
-    kv_recv, kv_up, kv_down, kv_side, kv_core,
-    at_recv, at_up, at_down, at_side, at_core,
+    kv_recv, kv_up, kv_down, kv_side, kv_core, kv_cross,
+    at_recv, at_up, at_down, at_side, at_core, at_cross,
     sum_send, sum_recv, local,
 ):
     t = lax.axis_index("tok")
@@ -81,7 +81,10 @@
             device_id=(dev, y), device_id_type=MESH,
         )
 
-    def stage1(buf, recv, up, down, side, core, k, it, src=None, go=True):
+    def far(buf, it):
+        return B == 2 and it >= buf.shape[0] // 2
+
+    def stage1(buf, recv, up, down, side, core, cross, k, it, src=None, go=True):
         L = level(k)
         slot = tid(L, b, c)
         dst = buf.at[it, slot]
@@ -99,11 +102,18 @@
         def _():
             act(copy(src, dst, down.at[k, it], rs, tid(a - 1, b, c)))
 
-        for j in range(1, B):
-            act(copy(src, dst, side.at[k, it, j - 1], rs, tid(a, (b + j) % B, c)))
         act(copy(src, dst, core.at[k, it, 0], rs, tid(a, b, 1 - c)))
 
-    def stage2(buf, recv, up, down, side, core, k, it, go=True):
+        def to_sides():
+            for j in range(1, B):
+                act(copy(src, dst, side.at[k, it, j - 1], rs, tid(a, (b + j) % B, c)))
+
+        if k > 0 and far(buf, it):
+            pl.when(L % (LEVELS - 1) != 0)(to_sides)
+        else:
+            to_sides()
+
+    def stage2(buf, recv, up, down, side, core, cross, k, it, go=True):
         L = level(k)
         for j in range(1, B):
             slot = tid(L, (b + j) % B, c)
@@ -116,8 +126,21 @@
                 d.start()
             else:
                 d.wait_send()
-
-    def stage3(buf, recv, up, down, side, core, k, it):
+            if far(buf, it):
+                for end, ahead, step in ((0, a < LEVELS - 1, 1), (LEVELS - 1, a > 0, -1)):
+
+                    @pl.when(jnp.logical_and(L == end, ahead))
+                    def _():
+                        onward = copy(
+                            buf.at[it, slot], buf.at[it, slot], cross.at[k, it],
+                            recv.at[it, slot], tid(a + step, b, c),
+                        )
+                        if go:
+                            onward.start()
+                        else:
+                            onward.wait_send()
+
+    def stage3(buf, recv, up, down, side, core, cross, k, it):
         L = level(k)
         for j in range(B):
             slot = tid(L, (b + j) % B, 1 - c)
@@ -126,8 +149,8 @@
                 recv.at[it, slot], tid(a, b, 1 - c),
             ).wait_recv()
 
-    kvs = (kv, kv_recv, kv_up, kv_down, kv_side, kv_core)
-    ats = (att, at_recv, at_up, at_down, at_side, at_core)
+    kvs = (kv, kv_recv, kv_up, kv_down, kv_side, kv_core, kv_cross)
+    ats = (att, at_recv, at_up, at_down, at_side, at_core, at_cross)
     own = (shared_k, shared_v)
 
     stage1(*kvs, 0, 0, shared_k)
@@ -257,8 +280,8 @@
         for i in range(per_level):
             p = piece(k, i)
             block = att[g, pl.ds(p * 4, 4)].reshape(4 * rows, gw)
-            part = jnp.dot(
-                block, w[g * gw : (g + 1) * gw, :], preferred_element_type=jnp.float32
+            part = lax.dot_general(
+                w[:, g * gw : (g + 1) * gw], block, contract, preferred_element_type=jnp.float32
             )
             if g > 0:
                 part = sums[i] + part
@@ -286,7 +309,10 @@
             stage3(*ats, *items[i - 3])
             project(*items[i - 3])
 
-    total = residual[...].astype(jnp.float32) + own_acc[...].reshape(residual.shape)
+    def across(sums_of):
+        return jnp.concatenate([sums_of(r).astype(jnp.float32) for r in range(share)], axis=1)
+
+    total = residual[...].astype(jnp.float32) + across(lambda r: own_acc[r])
     for j in range(1, M):
         other = (y + j) % M
         for r in range(share):
@@ -295,7 +321,7 @@
                 send_sem=sum_send.at[0], recv_sem=sum_recv.at[other, r],
                 device_id=(t, other), device_id_type=MESH,
             ).wait_recv()
-        total = total + in_sums[other].astype(jnp.float32).reshape(residual.shape)
+        total = total + across(lambda r: in_sums[other, r])
     hidden[...] = total.astype(jnp.bfloat16)
 
     for k in range(LEVELS):
@@ -310,6 +336,11 @@
             @pl.when(piece(k, i) // share != y)
             def _():
                 sum_copy(k, i).wait_send()
+
+
+def hand_over(*refs):
+    for source, target in zip(refs[:3], refs[3:]):
+        target[...] = source[...]
 
 
 def body(
@@ -323,7 +354,8 @@
     group = q_width // kv_width
     half = HEAD_SIZE // 2
     B = N // (2 * LEVELS)
-    columns = weight.shape[1]
+    weight, residual = weight.T, residual.T
+    columns = weight.shape[0]
     pieces = N // 4
     per_level = pieces // LEVELS
     share = pieces // M
@@ -338,10 +370,10 @@
     def semaphores(items):
         return [
             dma((items, N)), dma((LEVELS, items)), dma((LEVELS, items)),
-            dma((LEVELS, items, B - 1)), dma((LEVELS, items, B)),
+            dma((LEVELS, items, B - 1)), dma((LEVELS, items, B)), dma((LEVELS, items)),
         ]
 
-    return pl.pallas_call(
+    hidden, leaf_k_out, leaf_v_out = pl.pallas_call(
         functools.partial(kernel, N, M),
         out_shape=(
             jax.ShapeDtypeStruct(residual.shape, bf16),
@@ -355,10 +387,10 @@
             pltpu.VMEM((heads, N, rows, group * HEAD_SIZE), bf16),
             pltpu.VMEM(weight.shape, bf16),
             pltpu.VMEM((heads, group * rows, HEAD_SIZE), bf16),
-            pltpu.VMEM((share, 4 * rows, columns), f32),
-            pltpu.VMEM((per_level, 4 * rows, columns), f32),
-            pltpu.VMEM((pieces, 4 * rows, columns), bf16),
-            pltpu.VMEM((M, share, 4 * rows, columns), bf16),
+            pltpu.VMEM((share, columns, 4 * rows), f32),
+            pltpu.VMEM((per_level, columns, 4 * rows), f32),
+            pltpu.VMEM((pieces, columns, 4 * rows), bf16),
+            pltpu.VMEM((M, share, columns, 4 * rows), bf16),
         ]
         + semaphores(2)
         + semaphores(heads)
@@ -370,6 +402,14 @@
         queries, fresh_k, fresh_v, leaf_k, leaf_v, shared_k, shared_v, weight, residual,
         freq, request, positions.reshape(1, rows), parents, lengths, owners,
     )
+    results = (hidden, leaf_k_out, leaf_v_out)
+    hidden, leaf_k_out, leaf_v_out = pl.pallas_call(
+        hand_over,
+        out_shape=[jax.ShapeDtypeStruct(r.shape, r.dtype) for r in results],
+        in_specs=[vmem] * 3,
+        out_specs=[vmem] * 3,
+    )(*results)
+    return hidden.T, leaf_k_out, leaf_v_out
 
 
 def solution(mesh):

time: 125 us -> 111 us (0.89)
  local copies, waits for them, and re-layouts: 13.2 us -> 0 us
    unnamed x4 -> x0, local copies, waits for them, and re-layouts: 11.2 us -> none
    pallas_call x1, Pallas kernels: 111 us -> 108 us  [body(): pl.pallas_call(functools.partial(kernel, N, M), out_shape=(jax.ShapeDtype...]
    pallas_call x0 -> x1, Pallas kernels: none -> 2.22 us  [body(): pl.pallas_call(hand_over, out_shape=[jax.ShapeDtypeStruct(r.shape, r.dtyp...]
    pallas_call x1 -> x0, local copies, waits for them, and re-layouts: 2 us -> none  [body(): pl.pallas_call(functools.partial(kernel, N, M), out_shape=(jax.ShapeDtype...]
where the time goes in v2:
time: 111 us
  Pallas kernels  111 us (100%)
    pallas_call x1, Pallas kernels, body(): pl.pallas_call(functools.partial(kernel, N, M), out_shape=(jax.ShapeDtype...  108 us

profile of v2, /device:TPU:0, one launch (start us, length us, event | category | flops | bytes accessed | tf_op | source)
XLA Modules:
  0.0 111.2 jit_solution(7006346614099053513)
XLA Ops:
  0.6 108.3 %shard_map.166 = (bf16[448,512]{1,0:T(8,128)(2,1)}, bf16[320,512]{1,0:T(8,128)(2,1)}, bf16[320,512]{1,0:T(8,128)(2,1)}) custom-call(bf16[64,3584]{1,0:T(8,128)(2,1)} %queries.1, bf16[64,512]{1,0:T(8,128)(2,1)} %fresh_k.1, bf16[64,512]{1,0:T(8,128)(2,1)} %fresh_v.1, bf16[320,512]{1,0:T(8,128)(2,1)} %leaf_k.1, bf16[320,512]{1,0:T(8,128)(2,1)} %leaf_v.1, ...), custom_call_target="tpu_custom_call" | custom-call | tf_op jit(solution)/shard_map/pallas_call | solution.py:376
  109.0 2.2 %shard_map.167 = (bf16[448,512]{1,0:T(8,128)(2,1)}, bf16[320,512]{1,0:T(8,128)(2,1)}, bf16[320,512]{1,0:T(8,128)(2,1)}) custom-call(bf16[448,512]{1,0:T(8,128)(2,1)} %get-tuple-element.9.refs_0_, bf16[320,512]{1,0:T(8,128)(2,1)} %get-tuple-element.10.refs_1_, bf16[320,512]{1,0:T(8,128)(2,1)} %get-tuple-element.11.refs_2_), custom_call_target="tpu_custom_call" | custom-call | tf_op jit(solution)/shard_map/pallas_call | solution.py:406
